TPU v7x, 32 devices: a whole 2x2x4 slice. The times are simulated.
32 devices in a mesh: strip: 32 (over z, y, x, core).
Axes of the slice: x: 2, y: 2, z: 4, core: 2. Of those that a mesh axis runs over, the one named last changes fastest.
Arguments:
- velocity: float32 [2, 128, 128, 768], P(None, None, 'strip'), may hold values from -100 to 100
Outputs:
- spatial_modes: float32 [128, 128, 768], P(None, 'strip')
- triangle: float32 [128, 128], replicated
All inputs are finite; a program needn't handle non-finite values.
Results may differ from a plain program's by a relative error of at most 0.000094.
Values sent between devices are 32-bit elements; how exact they have to be, the bound alone decides.
A program may use at most 128 MiB of HBM per device.

v0:
```python
import jax
import jax.numpy as jnp
from jax import lax
from jax.sharding import PartitionSpec as P


def extended(array, sides, width):
    for axis, dim in sides:
        size, length = (lax.axis_size(axis), array.shape[dim])
        up = [(i, (i + 1) % size) for i in range(size)]
        down = [(j, i) for i, j in up]
        last = lax.slice_in_dim(array, length - width, length, axis=dim)
        initial = lax.slice_in_dim(array, 0, width, axis=dim)
        before = lax.ppermute(last, axis, up)
        after = lax.ppermute(initial, axis, down)
        array = jnp.concatenate([before, array, after], axis=dim)
    return array


def along_second(field):
    return (
        8.0 * (jnp.roll(field, -1, 2) - jnp.roll(field, 1, 2))
        - (jnp.roll(field, -2, 2) - jnp.roll(field, 2, 2))
    ) / 12.0


def stencil_rows(padded, row_count):
    return 8.0 * (padded[:, 3 : row_count + 3] - padded[:, 1 : row_count + 1]) - (
        padded[:, 4 : row_count + 4] - padded[:, 0:row_count]
    )


def local(velocity):
    snap_count = velocity.shape[1]
    row_count = velocity.shape[2]
    col_count = velocity.shape[3]
    total_cells = row_count * lax.axis_size("strip") * col_count
    comp_u = velocity[0]
    comp_v = velocity[1]
    padded = extended(comp_v, (("strip", 1),), 2)
    v_first = stencil_rows(padded, row_count) / 12.0
    vorticity = v_first - along_second(comp_u)
    flattened = vorticity.reshape(snap_count, row_count * col_count)
    local_gram = (
        jnp.dot(
            flattened,
            flattened.T,
            precision=lax.Precision.HIGHEST,
            preferred_element_type=jnp.float32,
        )
        / total_cells
    )
    gram = lax.psum(local_gram, "strip")
    lower = jnp.linalg.cholesky(gram)
    identity = jnp.eye(snap_count, dtype=jnp.float32)
    inverse_lower = lax.linalg.triangular_solve(lower, identity, left_side=True, lower=True)
    spatial_modes = jnp.dot(
        inverse_lower,
        flattened,
        precision=lax.Precision.HIGHEST,
        preferred_element_type=jnp.float32,
    )
    return (spatial_modes.reshape(snap_count, row_count, col_count), lower.T)


def solution(mesh):
    return jax.shard_map(
        local,
        mesh=mesh,
        in_specs=(P(None, None, "strip", None),),
        out_specs=(P(None, "strip", None), P()),
        check_vma=False,
    )
```

profile of v0, /device:TPU:0, one launch (start us, length us, event | category | flops | bytes accessed | tf_op | source)
XLA Modules:
  0.0 194.0 jit_solution(9467097260490297088)
XLA Ops:
  7.2 2.4 %slice_bitcast_fusion = (f32[128,4,768]{2,1,0:T(4,128)S(1)}, f32[128,4,768]{2,1,0:T(4,128)S(1)}) fusion(f32[2,128,4,768]{3,2,1,0:T(4,128)} %param.1), kind=kLoop, calls=%fused_computation.21 | loop fusion | bytes 6291456 | tf_op jit(solution)/shard_map/squeeze | solution.py:38
  9.6 0.6 fusion.26
  10.2 6.4 %collective-permute-start = (f32[128,2,768]{2,1,0:T(2,128)S(1)}, f32[128,2,768]{2,1,0:T(2,128)S(1)}, u32[]{:S(2)}, u32[]{:S(2)}) collective-permute-start(f32[128,2,768]{2,1,0:T(2,128)S(1)} %get-tuple-element.14), channel_id=1, source_target_pairs={{1,0},{2,1},{3,2},{4,3},{5,4},{6,5},{7,6},{8,7},{9,8},{10,9},{11,1... | collective-permute-start | bytes 2359304 | tf_op jit(solution)/shard_map/ppermute | solution.py:15
  16.7 0.2 fusion.24
  16.9 0.2 fusion.22
  17.1 0.9 fusion.25
  18.0 0.9 fusion.23
  18.9 7.3 %collective-permute-done = f32[128,2,768]{2,1,0:T(2,128)S(1)} collective-permute-done((f32[128,2,768]{2,1,0:T(2,128)S(1)}, f32[128,2,768]{2,1,0:T(2,128)S(1)}, u32[]{:S(2)}, u32[]{:S(2)}) %collective-permute-start) | collective-permute-done | bytes 786464 | tf_op jit(solution)/shard_map/ppermute | solution.py:15
  26.2 5.6 %collective-permute-done.1 = f32[128,2,768]{2,1,0:T(2,128)S(1)} collective-permute-done((f32[128,2,768]{2,1,0:T(2,128)S(1)}, f32[128,2,768]{2,1,0:T(2,128)S(1)}, u32[]{:S(2)}, u32[]{:S(2)}) %collective-permute-start.1) | collective-permute-done | bytes 786464 | tf_op jit(solution)/shard_map/ppermute | solution.py:14
  31.8 5.1 %fusion.5 = f32[128,4,768]{2,1,0:T(4,128)S(1)} fusion(f32[128,2,768]{2,1,0:T(2,128)S(1)} %collective-permute-done.1, f32[128,4,768]{2,1,0:T(4,128)S(1)} %get-tuple-element.5, f32[128,2,768]{2,1,0:T(2,128)S(1)} %collective-permute-done, f32[128,4,1]{2,1,0:T(4,128)S(1)} %get-tuple-element.11, f32[128,4,767]{2,1,0:T(4,128)S(1)} %get-tuple-element.13, ...), kind=kLoop, calls=%fused_computation.9 | loop fusion | flops 7471104 | bytes 11010048 | tf_op jit(solution)/shard_map/sub | solution.py:42
  36.9 2.3 %fusion.16 = f32[128,128]{0,1:T(8,128)} fusion(f32[128,4,768]{2,1,0:T(4,128)S(1)} %fusion.5), kind=kOutput, calls=%fused_computation.25 | convolution fusion | flops 603996160 | bytes 1638400 | tf_op jit(solution)/shard_map/dot_general | solution.py:45
  39.2 0.3 copy.12
  39.5 0.5 copy.7
  40.0 117.9 %all-reduce.2.cloned.1.call-done = f32[128,128]{0,1:T(8,128)} async-done(((f32[128,128]{0,1:T(8,128)}), f32[128,128]{0,1:T(8,128)}) %all-reduce.2.cloned.1.call-update) | async-done | bytes 65552 | tf_op jit(solution)/shard_map/psum | solution.py:53
  157.9 0.9 copy.6
  158.8 0.9 fusion.20
  159.7 11.7 %cholesky.17 = f32[128,128]{1,0:T(8,128)S(1)} custom-call(f32[128,128]{1,0:T(8,128)S(1)} %fusion.20), custom_call_target="Cholesky" | custom-call | tf_op jit(solution)/shard_map/jit(cholesky)/cholesky | solution.py:54
  171.4 0.6 compare_reduce_fusion
  172.1 0.7 fusion.21
  172.8 9.8 %custom-call.6 = f32[1,128,128]{1,2,0:T(8,128)S(1)} custom-call(f32[1,128,128]{2,1,0:T(8,128)S(1)} %get-tuple-element.17), custom_call_target="InvertDiagBlocksLowerTriangular" | custom-call | tf_op jit(solution)/shard_map/triangular_solve | solution.py:56
  182.6 0.2 convolution_bitcast_fusion
  182.8 1.5 fusion.27
  184.3 2.2 %copy.8 = f32[128,4,768]{2,1,0:T(4,128)} copy(f32[128,4,768]{2,0,1:T(8,128)S(1)} %fusion.27) | data formatting | bytes 3145728
  186.5 0.7 copy.9
  (4 shorter events, 0.1 us)
Async XLA Ops:
  7.2 150.7 %all-reduce.2.cloned.1.call-start = ((), (), s32[]{:S(2)}) async-start(), calls=%async_computation | async-start | bytes 131072 | tf_op jit(solution)/shard_map/psum | solution.py:53
  10.2 15.9 %collective-permute-start = (f32[128,2,768]{2,1,0:T(2,128)S(1)}, f32[128,2,768]{2,1,0:T(2,128)S(1)}, u32[]{:S(2)}, u32[]{:S(2)}) collective-permute-start(f32[128,2,768]{2,1,0:T(2,128)S(1)} %get-tuple-element.14), channel_id=1, source_target_pairs={{1,0},{2,1},{3,2},{4,3},{5,4},{6,5},{7,6},{8,7},{9,8},{10,9},{11,1... | collective-permute-start | bytes 2359304 | tf_op jit(solution)/shard_map/ppermute | solution.py:15
  16.7 15.1 %collective-permute-start.1 = (f32[128,2,768]{2,1,0:T(2,128)S(1)}, f32[128,2,768]{2,1,0:T(2,128)S(1)}, u32[]{:S(2)}, u32[]{:S(2)}) collective-permute-start(f32[128,2,768]{2,1,0:T(2,128)S(1)} %get-tuple-element.15), channel_id=1, source_target_pairs={{0,1},{1,2},{2,3},{3,4},{4,5},{5,6},{6,7},{7,8},{8,9},{9,10},{10,1... | collective-permute-start | bytes 2359304 | tf_op jit(solution)/shard_map/ppermute | solution.py:14
Sparse Core Ops, SparseCore 0:
  39.3 118.5 all-reduce.1
where the time goes:
time: 195 us; the launch traced here: 194 us
  waiting for transfers between devices  131 us (67%)
  other arithmetic  28.8 us (15%)
  between operations  14.1 us (7%)
  local copies, waits for them, and re-layouts  9.78 us (5%)
  starting transfers between devices  6.46 us (3%)
  matrix products  4.06 us (2%)
    psum x1, waiting for transfers between devices, local(): gram = lax.psum(local_gram, 'strip')  118 us
    another operation x3, other arithmetic, local(): lower = jnp.linalg.cholesky(gram)  12.4 us
    another operation x1, other arithmetic, local(): lax.linalg.triangular_solve(lower, identity, left_side=True, lower=True)  9.81 us
    ppermute x1, waiting for transfers between devices, extended(): after = lax.ppermute(initial, axis, down)  7.28 us
    ppermute x1, starting transfers between devices, extended(): after = lax.ppermute(initial, axis, down)  6.42 us
    ppermute x1, waiting for transfers between devices, extended(): before = lax.ppermute(last, axis, up)  5.61 us
    sub x1, other arithmetic, local(): vorticity = v_first - along_second(comp_u)  5.06 us
  transfers between devices with their start and end apart: 3, of which 3 were waited for; matrix products, arithmetic and copies ran while one was open for 2% of the time, Pallas kernels for 0%

commit v1 on v0

v1 whole, which is shorter than its diff:
```python
import functools

import jax
import jax.numpy as jnp
from jax import lax
from jax.experimental import pallas as pl
from jax.experimental.pallas import tpu as pltpu
from jax.sharding import PartitionSpec as P

LANES = 128
HIGHEST = lax.Precision.HIGHEST
MESH = pl.DeviceIdType.MESH


def gram_kernel(
    n, snaps, rows, chunks, group, scale,
    vel_ref, w_ref, gram_ref,
    vel, field, before, after, part, piece, gathered,
    load_sem, up_send, up_recv, down_send, down_recv,
    scatter_send, scatter_recv, cross_send, cross_recv, gather_send, gather_recv,
):
    me = lax.axis_index("strip")
    right, left = lax.rem(me + 1, n), lax.rem(me + n - 1, n)
    in_group = lax.rem(me, group)
    base = me - in_group
    group_id = me // group
    groups = n // group
    height = snaps // group
    stride = rows * chunks

    loads = [
        pltpu.make_async_copy(vel_ref.at[c], vel.at[c], load_sem.at[c]) for c in (1, 0)
    ]
    for load in loads:
        load.start()

    def group_peer(offset):
        return base + lax.rem(in_group + offset, group)

    def cross_peer(offset):
        return lax.rem(me + offset * group, n)

    barrier = pltpu.get_barrier_semaphore()
    greeted = [right, left]
    greeted += [group_peer(o) for o in range(1, group)]
    greeted += [cross_peer(o) for o in range(1, groups)]
    for peer in greeted:
        pl.semaphore_signal(barrier, inc=1, device_id=(peer,), device_id_type=MESH)
    loads[0].wait()
    for t in range(chunks):
        for r in range(rows):
            field[t, r] = vel[1, pl.ds(t * rows + r, snaps, stride=stride), :]
        if t == 0:
            pl.semaphore_wait(barrier, len(greeted))
        for src, dst, peer, send, recv in (
            (field.at[t, pl.ds(rows - 2, 2)], before.at[t], right, up_send, up_recv),
            (field.at[t, pl.ds(0, 2)], after.at[t], left, down_send, down_recv),
        ):
            pltpu.make_async_remote_copy(
                src_ref=src, dst_ref=dst, send_sem=send.at[t], recv_sem=recv.at[t],
                device_id=(peer,), device_id_type=MESH,
            ).start()

    loads[1].wait()
    step = 16
    cols = chunks * LANES

    @pl.loop(0, snaps // step)
    def _(block):
        first = block * step
        for r in range(rows):
            row = jnp.concatenate(
                [
                    vel[0, pl.ds(first * stride + t * rows + r, step, stride=stride), :]
                    for t in range(chunks)
                ],
                axis=1,
            )
            wide = row - pltpu.roll(row, 2, 1)
            nine = 8.0 * wide - pltpu.roll(wide, cols - 1, 1)
            along = pltpu.roll(nine, cols - 1, 1) - wide
            for t in range(chunks):
                here = pl.ds(first, step)
                out = -along[:, t * LANES : (t + 1) * LANES]
                for shift, weight in ((1, 8.0), (-1, -8.0), (2, -1.0), (-2, 1.0)):
                    if 0 <= r + shift < rows:
                        out = out + weight * field[t, r + shift, here]
                w_ref[t, r, here] = out

    for t in range(chunks):
        up = pltpu.make_async_remote_copy(
            src_ref=field.at[t, pl.ds(rows - 2, 2)], dst_ref=before.at[t],
            send_sem=up_send.at[t], recv_sem=up_recv.at[t],
            device_id=(right,), device_id_type=MESH,
        )
        down = pltpu.make_async_remote_copy(
            src_ref=field.at[t, pl.ds(0, 2)], dst_ref=after.at[t],
            send_sem=down_send.at[t], recv_sem=down_recv.at[t],
            device_id=(left,), device_id_type=MESH,
        )
        up.wait()
        down.wait()
        for r in range(rows):
            out = w_ref[t, r]
            for shift, weight in ((1, 8.0), (-1, -8.0), (2, -1.0), (-2, 1.0)):
                if r + shift < 0:
                    out = out + weight * before[t, r + shift + 2]
                elif r + shift >= rows:
                    out = out + weight * after[t, r + shift - rows]
            w_ref[t, r] = out
            term = lax.dot_general(
                out, out, (((1,), (1,)), ((), ())),
                precision=HIGHEST, preferred_element_type=jnp.float32,
            )
            if t == 0 and r == 0:
                part[...] = term
            else:
                part[...] += term

    copies = []
    for o in range(1, group):
        other = lax.rem(in_group + o, group)
        copy = pltpu.make_async_remote_copy(
            src_ref=part.at[pl.ds(pl.multiple_of(other * height, 8), height)],
            dst_ref=piece.at[o - 1],
            send_sem=scatter_send.at[o - 1], recv_sem=scatter_recv.at[o - 1],
            device_id=(group_peer(o),), device_id_type=MESH,
        )
        copy.start()
        copies.append(copy)
    mine = pl.ds(pl.multiple_of(in_group * height, 8), height)
    total = part[mine, :]
    for o in range(1, group):
        copies[o - 1].wait()
        total = total + piece[o - 1]
    if groups > 1:
        gathered[group_id] = total
        copies = []
        for o in range(1, groups):
            copy = pltpu.make_async_remote_copy(
                src_ref=gathered.at[group_id], dst_ref=gathered.at[group_id],
                send_sem=cross_send.at[o - 1], recv_sem=cross_recv.at[o - 1],
                device_id=(cross_peer(o),), device_id_type=MESH,
            )
            copy.start()
            copies.append(copy)
        for copy in copies:
            copy.wait()
        total = gathered[0]
        for g in range(1, groups):
            total = total + gathered[g]
    gram_ref[mine, :] = total * scale
    copies = []
    for o in range(1, group):
        copy = pltpu.make_async_remote_copy(
            src_ref=gram_ref.at[mine], dst_ref=gram_ref.at[mine],
            send_sem=gather_send.at[o - 1], recv_sem=gather_recv.at[o - 1],
            device_id=(group_peer(o),), device_id_type=MESH,
        )
        copy.start()
        copies.append(copy)
    for copy in copies:
        copy.wait()


def tiles_first(array):
    *lead, rows, cols = array.shape
    array = array.reshape(*lead, rows, cols // LANES, LANES)
    array = jnp.swapaxes(array, -3, -2)
    return array


def vorticity_gram(velocity, n):
    _, snaps, rows, cols = velocity.shape
    chunks = cols // LANES
    group = 8
    groups = n // group
    height = snaps // group
    scale = 1.0 / (144.0 * n * rows * cols)
    flat = tiles_first(velocity).reshape(2, snaps * chunks * rows, LANES)
    dma = pltpu.SemaphoreType.DMA
    f32 = jnp.float32
    vmem = pl.BlockSpec(memory_space=pltpu.VMEM)
    return pl.pallas_call(
        functools.partial(gram_kernel, n, snaps, rows, chunks, group, scale),
        out_shape=(
            jax.ShapeDtypeStruct((chunks, rows, snaps, LANES), f32),
            jax.ShapeDtypeStruct((snaps, snaps), f32),
        ),
        in_specs=[pl.BlockSpec(memory_space=pl.ANY)],
        out_specs=(vmem, vmem),
        scratch_shapes=[
            pltpu.VMEM((2, snaps * chunks * rows, LANES), f32),
            pltpu.VMEM((chunks, rows, snaps, LANES), f32),
            pltpu.VMEM((chunks, 2, snaps, LANES), f32),
            pltpu.VMEM((chunks, 2, snaps, LANES), f32),
            pltpu.VMEM((snaps, snaps), f32),
            pltpu.VMEM((group - 1, height, snaps), f32),
            pltpu.VMEM((groups, height, snaps), f32),
            dma((2,)),
            dma((chunks,)), dma((chunks,)), dma((chunks,)), dma((chunks,)),
            dma((group - 1,)), dma((group - 1,)),
            dma((max(groups - 1, 1),)), dma((max(groups - 1, 1),)),
            dma((group - 1,)), dma((group - 1,)),
        ],
        compiler_params=pltpu.CompilerParams(
            collective_id=0, has_side_effects=True, vmem_limit_bytes=32 * 1024 * 1024
        ),
        name="vorticity_gram",
    )(flat)


def local(n, velocity):
    _, snaps, rows, cols = velocity.shape
    chunks = cols // LANES
    w, gram = vorticity_gram(velocity, n)
    lower = jnp.linalg.cholesky(gram)
    identity = jnp.eye(snaps, dtype=jnp.float32)
    inverse = lax.linalg.triangular_solve(lower, identity, left_side=True, lower=True)
    modes = lax.dot_general(
        inverse * (1.0 / 12.0), w, (((1,), (2,)), ((), ())),
        precision=HIGHEST, preferred_element_type=jnp.float32,
    )
    modes = jnp.transpose(modes, (0, 2, 1, 3)).reshape(snaps, rows, cols)
    return modes, lower.T


def solution(mesh):
    return jax.shard_map(
        functools.partial(local, mesh.shape["strip"]),
        mesh=mesh,
        in_specs=(P(None, None, "strip", None),),
        out_specs=(P(None, "strip", None), P()),
        check_vma=False,
    )
```

time: 195 us -> 76.1 us (0.39)
  waiting for transfers between devices: 131 us -> 0 us
  Pallas kernels: 0 us -> 36 us
  between operations: 14.1 us -> 0.71 us
  starting transfers between devices: 6.46 us -> 0 us
  other arithmetic: 28.8 us -> 22.9 us
  local copies, waits for them, and re-layouts: 9.78 us -> 11.9 us
    psum x1 -> x0, waiting for transfers between devices: 118 us -> none  [local(): gram = lax.psum(local_gram, 'strip')]
    pallas_call x0 -> x1, Pallas kernels: none -> 36 us  [vorticity_gram(): pl.pallas_call(functools.partial(gram_kernel, n, snaps, rows, chunks, gro...]
    ppermute x2 -> x0, waiting for transfers between devices: 12.9 us -> none  [the longest x1 7.28 us: extended(): after = lax.ppermute(initial, axis, down)]
    ppermute x2 -> x0, starting transfers between devices: 6.43 us -> none  [the longest x1 6.42 us: extended(): after = lax.ppermute(initial, axis, down)]
    unnamed x3 -> x5, local copies, waits for them, and re-layouts: 3.16 us -> 8.32 us
    sub x1 -> x0, other arithmetic: 5.06 us -> none  [local(): vorticity = v_first - along_second(comp_u)]
    transpose x0 -> x2, local copies, waits for them, and re-layouts: none -> 3.51 us  [the longest x1 3.36 us: tiles_first(): array = jnp.swapaxes(array, -3, -2)]
    slice x5 -> x0, local copies, waits for them, and re-layouts: 2.82 us -> none  [the longest x2 1.1 us: along_second(): jnp.roll(field, 2, 2)]
  transfers between devices with their start and end apart: 3 -> 0, of which waited for: 3 -> 0; matrix products, arithmetic and copies ran while one was open for 2% -> 0% of each run, Pallas kernels for 0% -> 0%
where the time goes in v1:
time: 76.1 us; the launch traced here: 75.8 us
  Pallas kernels  36 us (47%)
  other arithmetic  22.9 us (30%)
  local copies, waits for them, and re-layouts  11.9 us (16%)
  matrix products  4.28 us (6%)
    pallas_call x1, Pallas kernels, vorticity_gram(): pl.pallas_call(functools.partial(gram_kernel, n, snaps, rows, chunks, gro...  36 us
    another operation x3, other arithmetic, local(): lower = jnp.linalg.cholesky(gram)  12.4 us
    another operation x1, other arithmetic, local(): lax.linalg.triangular_solve(lower, identity, left_side=True, lower=True)  9.81 us
    unnamed x5, local copies, waits for them, and re-layouts  8.32 us
    dot_general x1, matrix products, local(): lax.dot_general(inverse * (1.0 / 12.0), w, (((1,), (2,)), ((), ())), prec...  4.03 us
    transpose x1, local copies, waits for them, and re-layouts, tiles_first(): array = jnp.swapaxes(array, -3, -2)  3.36 us

profile of v1, /device:TPU:0, one launch (start us, length us, event | category | flops | bytes accessed | tf_op | source)
XLA Modules:
  0.0 75.8 jit_solution(18059168342519622948)
XLA Ops:
  0.6 4.9 %copy.7 = f32[2,128,4,768]{1,3,2,0:T(8,128)} copy(f32[2,128,4,768]{3,2,1,0:T(4,128)} %param.1) | data formatting | bytes 6291456 | tf_op args[0]
  5.5 3.4 %copy.8 = f32[2,128,6,4,128]{4,3,2,1,0:T(4,128)S(1)} copy(f32[2,128,6,4,128]{1,4,2,3,0:T(8,128)} %bitcast.25) | data formatting | bytes 6291456 | tf_op jit(solution)/shard_map/transpose | solution.py:169
  8.9 36.0 %vorticity_gram.1 = (f32[6,4,128,128]{3,2,1,0:T(8,128)S(1)}, f32[128,128]{1,0:T(8,128)S(1)}) custom-call(f32[2,3072,128]{2,1,0:T(8,128)S(1)} %bitcast.24), custom_call_target="tpu_custom_call" | custom-call | tf_op jit(solution)/shard_map/vorticity_gram/pallas_call | solution.py:184
  44.9 0.0 copy-start
  45.0 1.1 %copy-done = f32[6,4,128,128]{3,2,1,0:T(8,128)} copy-done((f32[6,4,128,128]{3,2,1,0:T(8,128)}, f32[6,4,128,128]{3,2,1,0:T(8,128)S(1)}, u32[]{:S(2)}) %copy-start) | copy-done | bytes 1572888
  46.1 0.1 copy.9
  46.2 11.7 %cholesky.17 = f32[128,128]{1,0:T(8,128)S(1)} custom-call(f32[128,128]{1,0:T(8,128)S(1)} %fusion.2), custom_call_target="Cholesky" | custom-call | tf_op jit(solution)/shard_map/jit(cholesky)/cholesky | solution.py:217
  58.0 0.6 compare_reduce_fusion
  58.6 0.7 fusion.3
  59.3 0.7 copy.13
  60.0 9.8 %custom-call.6 = f32[1,128,128]{1,2,0:T(8,128)S(1)} custom-call(f32[1,128,128]{2,1,0:T(8,128)S(1)} %get-tuple-element.11), custom_call_target="InvertDiagBlocksLowerTriangular" | custom-call | tf_op jit(solution)/shard_map/triangular_solve | solution.py:219
  69.8 0.3 fusion
  70.1 4.0 %convolution_bitcast_fusion = f32[128,4,6,128]{0,3,1,2:T(8,128)S(1)} fusion(f32[128,128,1,1]{1,0,3,2:T(8,128)S(1)} %fusion, f32[6,4,128,128]{3,2,1,0:T(8,128)} %copy-done), kind=kOutput, calls=%fused_computation | convolution fusion | flops 603979776 | bytes 3211264 | tf_op jit(solution)/shard_map/dot_general | solution.py:220
  74.1 0.1 copy.11
  74.2 1.6 %copy.12 = f32[128,4,768]{2,1,0:T(4,128)} copy(f32[128,4,768]{0,2,1:T(8,128)S(1)} %bitcast.26) | data formatting | bytes 3145728
  (2 shorter events, 0.0 us)
Async XLA Ops:
  44.9 1.1 %copy-start = (f32[6,4,128,128]{3,2,1,0:T(8,128)}, f32[6,4,128,128]{3,2,1,0:T(8,128)S(1)}, u32[]{:S(2)}) copy-start(f32[6,4,128,128]{3,2,1,0:T(8,128)S(1)} %get-tuple-element.5) | copy-start | bytes 4718596

commit v2 on v1

--- a/solution.py
+++ b/solution.py
@@ -5,6 +5,7 @@
 from jax import lax
 from jax.experimental import pallas as pl
 from jax.experimental.pallas import tpu as pltpu
+from jax.experimental.layout import Layout, with_layout_constraint
 from jax.sharding import PartitionSpec as P
 
 LANES = 128
@@ -166,8 +167,10 @@
 def tiles_first(array):
     *lead, rows, cols = array.shape
     array = array.reshape(*lead, rows, cols // LANES, LANES)
-    array = jnp.swapaxes(array, -3, -2)
-    return array
+    k = len(lead)
+    order = tuple(range(k)) + (k + 1, k, k + 2)
+    array = with_layout_constraint(array, Layout(major_to_minor=order))
+    return jnp.swapaxes(array, -3, -2)
 
 
 def vorticity_gram(velocity, n):
@@ -204,25 +207,102 @@
             dma((group - 1,)), dma((group - 1,)),
         ],
         compiler_params=pltpu.CompilerParams(
-            collective_id=0, has_side_effects=True, vmem_limit_bytes=32 * 1024 * 1024
+            collective_id=0, has_side_effects=True, vmem_limit_bytes=58 * 1024 * 1024
         ),
         name="vorticity_gram",
     )(flat)
 
 
+def modes_kernel(
+    snaps, rows, chunks, parts, gram_ref, w_ref, out_ref, triangle_ref, inverse, out, out_sem
+):
+    blocks = snaps // 8
+    sub = lax.broadcasted_iota(jnp.int32, (8, snaps), 0)
+    lane = lax.broadcasted_iota(jnp.int32, (8, snaps), 1)
+    left = [gram_ref[pl.ds(8 * b, 8), :] for b in range(blocks)]
+    side = [jnp.where(lane == sub + 8 * b, 1.0, 0.0) for b in range(blocks)]
+
+    for b in range(blocks):
+        spread = [
+            [jnp.broadcast_to(left[i][:, 8 * b + k : 8 * b + k + 1], (8, snaps)) for k in range(8)]
+            for i in range(b, blocks)
+        ]
+        pivots = spread[0][0]
+        for k in range(8):
+            pivot = spread[0][k][k : k + 1, :]
+            inv = 1.0 / pivot
+            pivots = jnp.where(sub == k, spread[0][k], pivots)
+            row_left = left[b][k : k + 1, :]
+            row_side = side[b][k : k + 1, :]
+            row_spread = [spread[0][q][k : k + 1, :] for q in range(k + 1, 8)]
+            for i in range(b, blocks):
+                mult = spread[i - b][k] * inv
+                if i == b:
+                    mult = jnp.where(sub > k, mult, 0.0)
+                if i > b or k < 7:
+                    left[i] = left[i] - mult * row_left
+                    side[i] = side[i] - mult * row_side
+                    for q in range(k + 1, 8):
+                        spread[i - b][q] = spread[i - b][q] - mult * row_spread[q - k - 1]
+        root = lax.rsqrt(pivots)
+        here = pl.ds(8 * b, 8)
+        triangle_ref[here, :] = jnp.where(lane >= sub + 8 * b, left[b] * root, 0.0)
+        inverse[here, :] = side[b] * (root * (1.0 / 12.0))
+
+    size = snaps // parts
+    span = size * rows * chunks
+    copies = []
+    for p in range(parts):
+        mine = inverse[pl.ds(p * size, size), :]
+        for t in range(chunks):
+            for r in range(rows):
+                out[pl.ds(p * span + t * rows + r, size, stride=rows * chunks), :] = jnp.dot(
+                    mine, w_ref[t, r], precision=HIGHEST, preferred_element_type=jnp.float32
+                )
+        copy = pltpu.make_async_copy(
+            out.at[pl.ds(p * span, span)], out_ref.at[pl.ds(p * span, span)], out_sem.at[p]
+        )
+        copy.start()
+        copies.append(copy)
+    for copy in copies:
+        copy.wait()
+
+
+def modes_triangle(gram, w):
+    chunks, rows, snaps, _ = w.shape
+    parts = 2
+    f32 = jnp.float32
+    vmem = pl.BlockSpec(memory_space=pltpu.VMEM)
+    return pl.pallas_call(
+        functools.partial(modes_kernel, snaps, rows, chunks, parts),
+        out_shape=(
+            jax.ShapeDtypeStruct((snaps * chunks * rows, LANES), f32),
+            jax.ShapeDtypeStruct((snaps, snaps), f32),
+        ),
+        in_specs=[vmem, vmem],
+        out_specs=(pl.BlockSpec(memory_space=pl.ANY), vmem),
+        scratch_shapes=[
+            pltpu.VMEM((snaps, snaps), f32),
+            pltpu.VMEM((snaps * chunks * rows, LANES), f32),
+            pltpu.SemaphoreType.DMA((parts,)),
+        ],
+        compiler_params=pltpu.CompilerParams(vmem_limit_bytes=58 * 1024 * 1024),
+        name="modes_triangle",
+    )(gram, w)
+
+
+def rows_first(array, snaps, rows, chunks):
+    array = array.reshape(snaps, chunks, rows, LANES)
+    array = jnp.swapaxes(array, 1, 2)
+    array = with_layout_constraint(array, Layout(major_to_minor=(0, 2, 1, 3)))
+    return array.reshape(snaps, rows, chunks * LANES)
+
+
 def local(n, velocity):
     _, snaps, rows, cols = velocity.shape
-    chunks = cols // LANES
     w, gram = vorticity_gram(velocity, n)
-    lower = jnp.linalg.cholesky(gram)
-    identity = jnp.eye(snaps, dtype=jnp.float32)
-    inverse = lax.linalg.triangular_solve(lower, identity, left_side=True, lower=True)
-    modes = lax.dot_general(
-        inverse * (1.0 / 12.0), w, (((1,), (2,)), ((), ())),
-        precision=HIGHEST, preferred_element_type=jnp.float32,
-    )
-    modes = jnp.transpose(modes, (0, 2, 1, 3)).reshape(snaps, rows, cols)
-    return modes, lower.T
+    modes, triangle = modes_triangle(gram, w)
+    return rows_first(modes, snaps, rows, cols // LANES), triangle
 
 
 def solution(mesh):

time: 76.1 us -> 46.6 us (0.61)
  other arithmetic: 22.9 us -> 0 us
  local copies, waits for them, and re-layouts: 11.9 us -> 0 us
  Pallas kernels: 36 us -> 45.8 us
  matrix products: 4.28 us -> 0 us
    another operation x4 -> x0, other arithmetic: 22.2 us -> none  [the longest x3 12.4 us: local(): lower = jnp.linalg.cholesky(gram)]
    pallas_call x0 -> x1, Pallas kernels: none -> 8.81 us  [modes_triangle(): pl.pallas_call(functools.partial(modes_kernel, snaps, rows, chunks, parts...]
    unnamed x5 -> x0, local copies, waits for them, and re-layouts: 8.32 us -> none
    dot_general x1 -> x0, matrix products: 4.03 us -> none  [local(): lax.dot_general(inverse * (1.0 / 12.0), w, (((1,), (2,)), ((), ())), prec...]
    transpose x2 -> x0, local copies, waits for them, and re-layouts: 3.51 us -> none  [the longest x1 3.36 us: tiles_first(): array = jnp.swapaxes(array, -3, -2)]
    pallas_call x1, Pallas kernels: 36 us -> 37 us  [vorticity_gram(): pl.pallas_call(functools.partial(gram_kernel, n, snaps, rows, chunks, gro...]
where the time goes in v2:
time: 46.6 us; the launch traced here: 46.4 us
  Pallas kernels  45.8 us (98%)
  between operations  0.64 us (1%)
    pallas_call x1, Pallas kernels, vorticity_gram(): pl.pallas_call(functools.partial(gram_kernel, n, snaps, rows, chunks, gro...  37 us
    pallas_call x1, Pallas kernels, modes_triangle(): pl.pallas_call(functools.partial(modes_kernel, snaps, rows, chunks, parts...  8.81 us

profile of v2, /device:TPU:0, one launch (start us, length us, event | category | flops | bytes accessed | tf_op | source)
XLA Modules:
  0.0 46.4 jit_solution(9503765571268785970)
XLA Ops:
  0.6 37.0 %vorticity_gram.1 = (f32[6,4,128,128]{3,2,1,0:T(8,128)}, f32[128,128]{1,0:T(8,128)}) custom-call(f32[2,3072,128]{2,1,0:T(8,128)} %bitcast.10), custom_call_target="tpu_custom_call" | custom-call | tf_op jit(solution)/shard_map/vorticity_gram/pallas_call | solution.py:187
  37.6 8.8 %modes_triangle.1 = (f32[3072,128]{1,0:T(8,128)}, f32[128,128]{1,0:T(8,128)}) custom-call(f32[128,128]{1,0:T(8,128)} %get-tuple-element.6.gram_ref, f32[6,4,128,128]{3,2,1,0:T(8,128)} %get-tuple-element.7.w_ref), custom_call_target="tpu_custom_call" | custom-call | tf_op jit(solution)/shard_map/modes_triangle/pallas_call | solution.py:276

commit v3 on v2

--- a/solution.py
+++ b/solution.py
@@ -9,15 +9,16 @@
 from jax.sharding import PartitionSpec as P
 
 LANES = 128
+GROUP = 8
 HIGHEST = lax.Precision.HIGHEST
 MESH = pl.DeviceIdType.MESH
 
 
 def gram_kernel(
     n, snaps, rows, chunks, group, scale,
-    vel_ref, w_ref, gram_ref,
-    vel, field, before, after, part, piece, gathered,
-    load_sem, up_send, up_recv, down_send, down_recv,
+    vel_ref, w_out, gram_ref,
+    w_ref, vel, field, before, after, part, piece, gathered,
+    load_sem, w_sem, up_send, up_recv, down_send, down_recv,
     scatter_send, scatter_recv, cross_send, cross_recv, gather_send, gather_recv,
 ):
     me = lax.axis_index("strip")
@@ -26,14 +27,12 @@
     base = me - in_group
     group_id = me // group
     groups = n // group
-    height = snaps // group
     stride = rows * chunks
 
     loads = [
         pltpu.make_async_copy(vel_ref.at[c], vel.at[c], load_sem.at[c]) for c in (1, 0)
     ]
-    for load in loads:
-        load.start()
+    loads[0].start()
 
     def group_peer(offset):
         return base + lax.rem(in_group + offset, group)
@@ -61,6 +60,8 @@
                 src_ref=src, dst_ref=dst, send_sem=send.at[t], recv_sem=recv.at[t],
                 device_id=(peer,), device_id_type=MESH,
             ).start()
+        if t == 0:
+            loads[1].start()
 
     loads[1].wait()
     step = 16
@@ -88,6 +89,7 @@
                         out = out + weight * field[t, r + shift, here]
                 w_ref[t, r, here] = out
 
+    sent = []
     for t in range(chunks):
         up = pltpu.make_async_remote_copy(
             src_ref=field.at[t, pl.ds(rows - 2, 2)], dst_ref=before.at[t],
@@ -99,8 +101,9 @@
             send_sem=down_send.at[t], recv_sem=down_recv.at[t],
             device_id=(left,), device_id_type=MESH,
         )
-        up.wait()
-        down.wait()
+        up.wait_recv()
+        down.wait_recv()
+        sent += [up, down]
         for r in range(rows):
             out = w_ref[t, r]
             for shift, weight in ((1, 8.0), (-1, -8.0), (2, -1.0), (-2, 1.0)):
@@ -113,27 +116,26 @@
                 out, out, (((1,), (1,)), ((), ())),
                 precision=HIGHEST, preferred_element_type=jnp.float32,
             )
-            if t == 0 and r == 0:
-                part[...] = term
-            else:
-                part[...] += term
+            gram = term if t == 0 and r == 0 else gram + term
+        pltpu.make_async_copy(w_ref.at[t], w_out.at[t], w_sem.at[t]).start()
+    part[...] = gram.reshape(part.shape)
 
     copies = []
     for o in range(1, group):
         other = lax.rem(in_group + o, group)
         copy = pltpu.make_async_remote_copy(
-            src_ref=part.at[pl.ds(pl.multiple_of(other * height, 8), height)],
+            src_ref=part.at[other],
             dst_ref=piece.at[o - 1],
             send_sem=scatter_send.at[o - 1], recv_sem=scatter_recv.at[o - 1],
             device_id=(group_peer(o),), device_id_type=MESH,
         )
         copy.start()
         copies.append(copy)
-    mine = pl.ds(pl.multiple_of(in_group * height, 8), height)
-    total = part[mine, :]
+    total = part[in_group]
     for o in range(1, group):
-        copies[o - 1].wait()
+        copies[o - 1].wait_recv()
         total = total + piece[o - 1]
+    sent += copies
     if groups > 1:
         gathered[group_id] = total
         copies = []
@@ -146,22 +148,27 @@
             copy.start()
             copies.append(copy)
         for copy in copies:
-            copy.wait()
+            copy.wait_recv()
+        sent += copies
         total = gathered[0]
         for g in range(1, groups):
             total = total + gathered[g]
-    gram_ref[mine, :] = total * scale
+    gram_ref[in_group] = total * scale
     copies = []
     for o in range(1, group):
         copy = pltpu.make_async_remote_copy(
-            src_ref=gram_ref.at[mine], dst_ref=gram_ref.at[mine],
+            src_ref=gram_ref.at[in_group], dst_ref=gram_ref.at[in_group],
             send_sem=gather_send.at[o - 1], recv_sem=gather_recv.at[o - 1],
             device_id=(group_peer(o),), device_id_type=MESH,
         )
         copy.start()
         copies.append(copy)
     for copy in copies:
-        copy.wait()
+        copy.wait_recv()
+    for copy in sent + copies:
+        copy.wait_send()
+    for t in range(chunks):
+        pltpu.make_async_copy(w_ref.at[t], w_out.at[t], w_sem.at[t]).wait()
 
 
 def tiles_first(array):
@@ -176,7 +183,7 @@
 def vorticity_gram(velocity, n):
     _, snaps, rows, cols = velocity.shape
     chunks = cols // LANES
-    group = 8
+    group = GROUP if n % GROUP == 0 else 1
     groups = n // group
     height = snaps // group
     scale = 1.0 / (144.0 * n * rows * cols)
@@ -188,19 +195,20 @@
         functools.partial(gram_kernel, n, snaps, rows, chunks, group, scale),
         out_shape=(
             jax.ShapeDtypeStruct((chunks, rows, snaps, LANES), f32),
-            jax.ShapeDtypeStruct((snaps, snaps), f32),
+            jax.ShapeDtypeStruct((group, height, snaps), f32),
         ),
         in_specs=[pl.BlockSpec(memory_space=pl.ANY)],
-        out_specs=(vmem, vmem),
+        out_specs=(pl.BlockSpec(memory_space=pl.ANY), vmem),
         scratch_shapes=[
+            pltpu.VMEM((chunks, rows, snaps, LANES), f32),
             pltpu.VMEM((2, snaps * chunks * rows, LANES), f32),
             pltpu.VMEM((chunks, rows, snaps, LANES), f32),
             pltpu.VMEM((chunks, 2, snaps, LANES), f32),
             pltpu.VMEM((chunks, 2, snaps, LANES), f32),
-            pltpu.VMEM((snaps, snaps), f32),
+            pltpu.VMEM((group, height, snaps), f32),
             pltpu.VMEM((group - 1, height, snaps), f32),
             pltpu.VMEM((groups, height, snaps), f32),
-            dma((2,)),
+            dma((2,)), dma((chunks,)),
             dma((chunks,)), dma((chunks,)), dma((chunks,)), dma((chunks,)),
             dma((group - 1,)), dma((group - 1,)),
             dma((max(groups - 1, 1),)), dma((max(groups - 1, 1),)),
@@ -217,6 +225,9 @@
     snaps, rows, chunks, parts, gram_ref, w_ref, out_ref, triangle_ref, inverse, out, out_sem
 ):
     blocks = snaps // 8
+    size = snaps // parts
+    span = size * rows * chunks
+    copies = []
     sub = lax.broadcasted_iota(jnp.int32, (8, snaps), 0)
     lane = lax.broadcasted_iota(jnp.int32, (8, snaps), 1)
     left = [gram_ref[pl.ds(8 * b, 8), :] for b in range(blocks)]
@@ -249,21 +260,23 @@
         triangle_ref[here, :] = jnp.where(lane >= sub + 8 * b, left[b] * root, 0.0)
         inverse[here, :] = side[b] * (root * (1.0 / 12.0))
 
-    size = snaps // parts
-    span = size * rows * chunks
-    copies = []
-    for p in range(parts):
-        mine = inverse[pl.ds(p * size, size), :]
+        if (8 * b + 8) % size:
+            continue
+        p = b * 8 // size
+        known = (p + 1) * size
+        mine = inverse[pl.ds(p * size, size), :][:, :known]
         for t in range(chunks):
             for r in range(rows):
                 out[pl.ds(p * span + t * rows + r, size, stride=rows * chunks), :] = jnp.dot(
-                    mine, w_ref[t, r], precision=HIGHEST, preferred_element_type=jnp.float32
+                    mine, w_ref[t, r, pl.ds(0, known)],
+                    precision=HIGHEST, preferred_element_type=jnp.float32,
                 )
         copy = pltpu.make_async_copy(
             out.at[pl.ds(p * span, span)], out_ref.at[pl.ds(p * span, span)], out_sem.at[p]
         )
         copy.start()
         copies.append(copy)
+
     for copy in copies:
         copy.wait()
 
@@ -301,6 +314,7 @@
 def local(n, velocity):
     _, snaps, rows, cols = velocity.shape
     w, gram = vorticity_gram(velocity, n)
+    gram = gram.reshape(snaps, snaps)
     modes, triangle = modes_triangle(gram, w)
     return rows_first(modes, snaps, rows, cols // LANES), triangle
 

time: 46.6 us -> 46 us (0.987)
  Pallas kernels: 45.8 us -> 45.2 us
    pallas_call x1, Pallas kernels: 37 us -> 36.5 us  [vorticity_gram(): pl.pallas_call(functools.partial(gram_kernel, n, snaps, rows, chunks, gro...]
where the time goes in v3:
time: 46 us; the launch traced here: 45.8 us
  Pallas kernels  45.2 us (98%)
  between operations  0.64 us (1%)
    pallas_call x1, Pallas kernels, vorticity_gram(): pl.pallas_call(functools.partial(gram_kernel, n, snaps, rows, chunks, gro...  36.5 us
    pallas_call x1, Pallas kernels, modes_triangle(): pl.pallas_call(functools.partial(modes_kernel, snaps, rows, chunks, parts...  8.67 us

profile of v3, /device:TPU:0, one launch (start us, length us, event | category | flops | bytes accessed | tf_op | source)
XLA Modules:
  0.0 45.8 jit_solution(15194902170672263402)
XLA Ops:
  0.6 36.5 %vorticity_gram.1 = (f32[6,4,128,128]{3,2,1,0:T(8,128)}, f32[8,16,128]{2,1,0:T(8,128)}) custom-call(f32[2,3072,128]{2,1,0:T(8,128)} %bitcast.11), custom_call_target="tpu_custom_call" | custom-call | tf_op jit(solution)/shard_map/vorticity_gram/pallas_call | solution.py:194
  37.2 8.7 %modes_triangle.1 = (f32[3072,128]{1,0:T(8,128)}, f32[128,128]{1,0:T(8,128)}) custom-call(f32[128,128]{1,0:T(8,128)} %bitcast.12, f32[6,4,128,128]{3,2,1,0:T(8,128)} %get-tuple-element.7.w_ref), custom_call_target="tpu_custom_call" | custom-call | tf_op jit(solution)/shard_map/modes_triangle/pallas_call | solution.py:289

commit v4 on v3

--- a/solution.py
+++ b/solution.py
@@ -10,6 +10,7 @@
 
 LANES = 128
 GROUP = 8
+SLABS = 4
 HIGHEST = lax.Precision.HIGHEST
 MESH = pl.DeviceIdType.MESH
 
@@ -29,10 +30,20 @@
     groups = n // group
     stride = rows * chunks
 
+    slab = snaps * stride // SLABS
     loads = [
-        pltpu.make_async_copy(vel_ref.at[c], vel.at[c], load_sem.at[c]) for c in (1, 0)
+        [
+            pltpu.make_async_copy(
+                vel_ref.at[c, pl.ds(i * slab, slab)],
+                vel.at[c, pl.ds(i * slab, slab)],
+                load_sem.at[c, i],
+            )
+            for i in range(SLABS)
+        ]
+        for c in (1, 0)
     ]
-    loads[0].start()
+    for load in loads[0]:
+        load.start()
 
     def group_peer(offset):
         return base + lax.rem(in_group + offset, group)
@@ -46,7 +57,8 @@
     greeted += [cross_peer(o) for o in range(1, groups)]
     for peer in greeted:
         pl.semaphore_signal(barrier, inc=1, device_id=(peer,), device_id_type=MESH)
-    loads[0].wait()
+    for load in loads[0]:
+        load.wait()
     for t in range(chunks):
         for r in range(rows):
             field[t, r] = vel[1, pl.ds(t * rows + r, snaps, stride=stride), :]
@@ -61,9 +73,11 @@
                 device_id=(peer,), device_id_type=MESH,
             ).start()
         if t == 0:
-            loads[1].start()
-
-    loads[1].wait()
+            for load in loads[1]:
+                load.start()
+
+    for load in loads[1]:
+        load.wait()
     step = 16
     cols = chunks * LANES
 
@@ -208,7 +222,7 @@
             pltpu.VMEM((group, height, snaps), f32),
             pltpu.VMEM((group - 1, height, snaps), f32),
             pltpu.VMEM((groups, height, snaps), f32),
-            dma((2,)), dma((chunks,)),
+            dma((2, SLABS)), dma((chunks,)),
             dma((chunks,)), dma((chunks,)), dma((chunks,)), dma((chunks,)),
             dma((group - 1,)), dma((group - 1,)),
             dma((max(groups - 1, 1),)), dma((max(groups - 1, 1),)),

time: 46 us -> 46.1 us (level)
  no operation moved by 1% of the time
where the time goes in v4:
time: 46.1 us; the launch traced here: 45.9 us
  Pallas kernels  45.3 us (98%)
  between operations  0.64 us (1%)
    pallas_call x1, Pallas kernels, vorticity_gram(): pl.pallas_call(functools.partial(gram_kernel, n, snaps, rows, chunks, gro...  36.6 us
    pallas_call x1, Pallas kernels, modes_triangle(): pl.pallas_call(functools.partial(modes_kernel, snaps, rows, chunks, parts...  8.67 us

profile of v4, /device:TPU:0, one launch (start us, length us, event | category | flops | bytes accessed | tf_op | source)
XLA Modules:
  0.0 45.9 jit_solution(7660171693944905384)
XLA Ops:
  0.6 36.6 %vorticity_gram.1 = (f32[6,4,128,128]{3,2,1,0:T(8,128)}, f32[8,16,128]{2,1,0:T(8,128)}) custom-call(f32[2,3072,128]{2,1,0:T(8,128)} %bitcast.11), custom_call_target="tpu_custom_call" | custom-call | tf_op jit(solution)/shard_map/vorticity_gram/pallas_call | solution.py:208
  37.2 8.7 %modes_triangle.1 = (f32[3072,128]{1,0:T(8,128)}, f32[128,128]{1,0:T(8,128)}) custom-call(f32[128,128]{1,0:T(8,128)} %bitcast.12, f32[6,4,128,128]{3,2,1,0:T(8,128)} %get-tuple-element.7.w_ref), custom_call_target="tpu_custom_call" | custom-call | tf_op jit(solution)/shard_map/modes_triangle/pallas_call | solution.py:303
